TPU v7x, 256 devices: a whole 4x4x8 slice. The times are simulated.
256 devices in a mesh: gx: 16 (over y, z_hi), gy: 4 (over x), gz: 4 (over z_lo, core).
Axes of the slice: x: 4, y: 4, z: 8 (z_hi: 4, z_lo: 2; z = z_hi * 2 + z_lo), core: 2. Of those that a mesh axis runs over, the one named last changes fastest.
Arguments:
- slab: float32 [672, 672, 512], P('gx', 'gy', 'gz'), may hold values from -36 to 36
- start_one: float32 [672, 96], replicated, may hold values from -6 to 6
- start_two: float32 [672, 96], replicated, may hold values from -6 to 6
Outputs:
- factor_one: float32 [672, 96], replicated
- factor_two: float32 [672, 96], replicated
- core: float32 [96, 96, 512], P('gx', 'gy', 'gz')
All inputs are finite; a program needn't handle non-finite values.
Results may differ from a plain program's by a relative error of at most 0.0003.
Values sent between devices are 32-bit elements; how exact they have to be, the bound alone decides.
A program may use at most 128 MiB of HBM per device.

v0:
```python
import jax
import jax.numpy as jnp
from jax import lax
from jax.sharding import PartitionSpec as P

ITERS = 8


precise = lax.Precision.HIGHEST


def orthonormal(matrix, inner_fn):
    square = inner_fn(jnp.dot(matrix.T, matrix, precision=precise))
    factor = jnp.linalg.cholesky(square)
    return lax.linalg.triangular_solve(
        factor, matrix, left_side=False, lower=True, transpose_a=True
    )


def keep_same(value):
    return value


def subspace(gram_rows, basis, inner_fn, collect_fn):
    for sweep_index in range(ITERS):
        rows_out = orthonormal(jnp.dot(gram_rows, basis, precision=precise), inner_fn)
        basis = collect_fn(rows_out)
    return basis


def body(slab, start_one, start_two):
    gy_count = lax.axis_size("gy")
    gz_count = lax.axis_size("gz")
    row_count, col_block, depth = slab.shape
    rank_total = start_one.shape[1]
    spread = lax.all_to_all(
        slab.reshape(row_count, col_block * depth), "gx", split_axis=1, concat_axis=0, tiled=True
    )
    partial_value = jnp.dot(spread, spread.T, precision=precise)
    scale_one = 1.0 / (col_block * gy_count * depth * gz_count)
    gram_one = lax.psum(partial_value, ("gx", "gy", "gz")) * scale_one
    factor_one = subspace(gram_one, start_one, keep_same, keep_same)
    own_first = lax.dynamic_slice_in_dim(factor_one, lax.axis_index("gx") * row_count, row_count, 0)
    partial_core = lax.psum_scatter(
        jnp.einsum("ir,ijc->rjc", own_first, slab, precision=precise),
        "gx",
        scatter_dimension=0,
        tiled=True,
    )
    spread_second = lax.all_to_all(partial_core, "gy", split_axis=2, concat_axis=1, tiled=True)
    partial_two = jnp.einsum("rjc,rkc->jk", spread_second, spread_second, precision=precise)
    scale_two = 1.0 / (rank_total * depth * gz_count)
    gram_two = lax.psum(partial_two, ("gx", "gy", "gz")) * scale_two
    factor_two = subspace(gram_two, start_two, keep_same, keep_same)
    own_second = lax.dynamic_slice_in_dim(
        factor_two, lax.axis_index("gy") * col_block, col_block, 0
    )
    core_terms = jnp.einsum("rjc,js->rsc", partial_core, own_second, precision=precise)
    core = lax.psum_scatter(core_terms, "gy", scatter_dimension=1, tiled=True)
    return (factor_one, factor_two, core)


def solution(mesh):
    placed = (P("gx", "gy", "gz"), P(), P())
    return jax.shard_map(
        body, mesh=mesh, in_specs=placed, out_specs=(P(), P(), P("gx", "gy", "gz")), check_vma=False
    )
```

profile of v0, /device:TPU:1, one launch (start us, length us, event | category | flops | bytes accessed | tf_op | source)
XLA Modules:
  0.0 1180.3 jit_solution(17631542794927374783)
XLA Ops:
  15.6 109.3 %all_to_all.37 = f32[42,16,1344]{2,0,1:T(8,128)} all-to-all(f32[42,16,1344]{2,0,1:T(8,128)S(1)} %copy.74), channel_id=1, replica_groups=mesh['gx'=16,'gy'=4,'gz'=4] {'gx'}, dimensions={1} | all-to-all | bytes 7225344 | tf_op jit(solution)/shard_map/all_to_all | solution.py:36
  128.7 14.6 %fusion.134 = f32[672,672]{1,0:T(8,128)} fusion(f32[672,1344]{1,0:T(8,128)} %all_to_all.30), kind=kOutput, calls=%fused_computation.211 | convolution fusion | flops 7283146752 | bytes 5419008 | tf_op jit(solution)/shard_map/dot_general | solution.py:39
  143.7 257.6 %all-reduce.3.cloned.1.call-done = f32[672,672]{1,0:T(8,128)} async-done(((f32[672,672]{1,0:T(8,128)}), f32[672,672]{1,0:T(8,128)}) %all-reduce.3.cloned.1.call-update) | async-done | bytes 1806352 | tf_op jit(solution)/shard_map/psum | solution.py:41
  405.6 8.8 cholesky.254
  426.0 8.8 cholesky.265
  446.6 8.8 cholesky.276
  467.1 8.8 cholesky.287
  487.8 8.8 cholesky.298
  508.2 8.8 cholesky.309
  529.1 8.8 cholesky.320
  549.6 8.8 cholesky.331
  567.7 9.1 fusion
  584.8 118.9 %reduce-scatter.3.cloned.1.call-done = f32[6,168,128]{2,1,0:T(8,128)} async-done(((f32[96,168,128]{2,1,0:T(8,128)}), f32[6,168,128]{2,1,0:T(8,128)}) %reduce-scatter.3.cloned.1.call-update) | async-done | bytes 516112 | tf_op jit(solution)/shard_map/reduce_scatter | solution.py:44
  706.2 10.8 all_to_all.38
  725.1 259.8 %all-reduce.5.cloned.1.call-done = f32[672,672]{1,0:T(8,128)} async-done(((f32[672,672]{1,0:T(8,128)}), f32[672,672]{1,0:T(8,128)}) %all-reduce.5.cloned.1.call-update) | async-done | bytes 1806352 | tf_op jit(solution)/shard_map/psum | solution.py:53
  989.1 8.8 cholesky.342
  1009.6 8.8 cholesky.353
  1030.2 8.8 cholesky.364
  1050.7 8.8 cholesky.375
  1071.6 8.8 cholesky.386
  1092.0 8.8 cholesky.397
  1112.6 8.8 cholesky.408
  1133.1 8.8 cholesky.419
  1152.2 21.4 %reduce-scatter.5.cloned.1.call-done = f32[6,24,128]{2,1,0:T(8,128)} async-done(((f32[6,96,128]{2,1,0:T(8,128)}), f32[6,24,128]{2,1,0:T(8,128)}) %reduce-scatter.5.cloned.1.call-update) | async-done | bytes 73744 | tf_op jit(solution)/shard_map/reduce_scatter | solution.py:59
  (179 shorter events, 223.6 us)
Async XLA Ops:
  7.2 394.2 %copy-start = (f32[672,96]{0,1:T(8,128)S(1)}, f32[672,96]{0,1:T(8,128)}, u32[]{:S(2)}) copy-start(f32[672,96]{0,1:T(8,128)} %param.7) | copy-start | bytes 774148
  7.2 394.1 %all-reduce.3.cloned.1.call-start = ((), (), s32[]{:S(2)}) async-start(), calls=%async_computation.4 | async-start | bytes 4128768 | tf_op jit(solution)/shard_map/psum | solution.py:41
  143.2 560.5 %reduce-scatter.3.cloned.1.call-start = ((), (), s32[]{:S(2)}) async-start(), calls=%async_computation.5 | async-start | bytes 8773632 | tf_op jit(solution)/shard_map/reduce_scatter | solution.py:44
  401.3 22.2 %copy-start.2 = (f32[672,672]{1,0:T(8,128)S(1)}, f32[672,672]{1,0:T(8,128)}, u32[]{:S(2)}) copy-start(f32[672,672]{1,0:T(8,128)} %all-reduce.3.cloned.1.call-done) | copy-start | bytes 5419012
  567.7 9.1 copy-start.5
  584.8 400.1 %all-reduce.5.cloned.1.call-start = ((), (), s32[]{:S(2)}) async-start(), calls=%async_computation.6 | async-start | bytes 4128768 | tf_op jit(solution)/shard_map/psum | solution.py:53
  724.6 260.3 %copy-start.6 = (f32[672,96]{0,1:T(8,128)S(1)}, f32[672,96]{0,1:T(8,128)}, u32[]{:S(2)}) copy-start(f32[672,96]{0,1:T(8,128)} %param.8) | copy-start | bytes 774148
  724.6 449.0 %reduce-scatter.5.cloned.1.call-start = ((), (), s32[]{:S(2)}) async-start(), calls=%async_computation.7 | async-start | bytes 368640 | tf_op jit(solution)/shard_map/reduce_scatter | solution.py:59
  984.9 22.2 %copy-start.1 = (f32[672,672]{1,0:T(8,128)S(1)}, f32[672,672]{1,0:T(8,128)}, u32[]{:S(2)}) copy-start(f32[672,672]{1,0:T(8,128)} %all-reduce.5.cloned.1.call-done) | copy-start | bytes 5419012
  1130.6 20.5 %copy-start.3 = (f32[6,168,128]{2,1,0:T(8,128)S(1)}, f32[6,168,128]{2,1,0:T(8,128)}, u32[]{:S(2)}) copy-start(f32[6,168,128]{2,1,0:T(8,128)} %reduce-scatter.3.cloned.1.call-done) | copy-start | bytes 1548292
  1151.0 22.6 %copy-start.4 = (f32[672,96]{0,1:T(8,128)}, f32[672,96]{0,1:T(8,128)S(1)}, u32[]{:S(2)}) copy-start(f32[672,96]{0,1:T(8,128)S(1)} %convolution_bitcast_fusion.2) | copy-start | bytes 774148
Sparse Core Ops, SparseCore 0:
  143.3 257.9 all-reduce.2
  584.9 118.7 reduce-scatter.2
  724.8 260.1 all-reduce.4
  1152.4 21.1 reduce-scatter.4
where the time goes:
time: 1190 us; the launch traced here: 1180 us
  waiting for transfers between devices  658 us (55%)
  other arithmetic  282 us (24%)
  blocking collectives  120 us (10%)
  matrix products  78.7 us (7%)
  local copies, waits for them, and re-layouts  26.2 us (2%)
  between operations  15 us (1%)
    psum x1, waiting for transfers between devices, body(): gram_two = lax.psum(partial_two, ('gx', 'gy', 'gz')) * scale_two  260 us
    psum x1, waiting for transfers between devices, body(): gram_one = lax.psum(partial_value, ('gx', 'gy', 'gz')) * scale_one  258 us
    another operation x48, other arithmetic, orthonormal(): factor = jnp.linalg.cholesky(square)  151 us
    another operation x32, other arithmetic, orthonormal(): lax.linalg.triangular_solve(factor, matrix, left_side=False, lower=True,...  128 us
    reduce_scatter x1, waiting for transfers between devices, body(): lax.psum_scatter(jnp.einsum('ir,ijc->rjc', own_first, slab, precision=pre...  119 us
    all_to_all x1, blocking collectives, body(): lax.all_to_all(slab.reshape(row_count, col_block * depth), 'gx', split_ax...  109 us
    dot_general x16, matrix products, subspace(): jnp.dot(gram_rows, basis, precision=precise)  35.5 us
  transfers between devices with their start and end apart: 4, of which 4 were waited for; matrix products, arithmetic and copies ran while one was open for 0% of the time, Pallas kernels for 0%

commit v1 on v0

v1 whole, which is shorter than its diff:
```python
import functools
import jax
import jax.numpy as jnp
from jax import lax
from jax.experimental import pallas as pl
from jax.experimental.pallas import tpu as pltpu
from jax.sharding import PartitionSpec as P

RANK = 96
ROWS = 672
ITERS = 8
OWN = 42
LANES = 128
MESH = pl.DeviceIdType.MESH
F32 = jnp.float32
BF16 = jnp.bfloat16
COUNT = (84, 68, 52, 36, 16)
BASE = (0, 84, 152, 204, 240)


def split(value):
    high = value.astype(BF16)
    low = (value - high.astype(F32)).astype(BF16)
    return high, low


def dot(a, b, left, right):
    return lax.dot_general(a, b, (((left,), (right,)), ((), ())), preferred_element_type=F32)


def nt(a, b):
    return dot(a, b, 1, 1)


def nn(a, b):
    return dot(a, b, 1, 0)


def vmem(count):
    return [pl.BlockSpec(memory_space=pltpu.VMEM)] * count


def inverse_factor(square):
    rows = [square[8 * t : 8 * t + 8, :] for t in range(12)]
    lane = lax.broadcasted_iota(jnp.int32, (8, 128), 1)
    sub = lax.broadcasted_iota(jnp.int32, (8, 128), 0)
    aside = [(lane == sub + 8 * t).astype(F32) for t in range(12)]
    done = []
    for t in range(12):
        first = 8 * t
        tile, extra = rows[t], aside[t]
        cell = {
            (j, l): jnp.broadcast_to(tile[j : j + 1, first + l : first + l + 1], (8, 128))
            for j in range(8)
            for l in range(j + 1)
        }
        line = [jnp.broadcast_to(tile[j : j + 1, :], (8, 128)) for j in range(8)]
        side = [jnp.broadcast_to(extra[j : j + 1, :], (8, 128)) for j in range(8)]
        inv = []
        for l in range(8):
            flip = 1.0 / cell[l, l]
            inv.append(flip)
            for j in range(l + 1, 8):
                times = cell[j, l] * flip
                for m in range(l + 1, j + 1):
                    cell[j, m] = cell[j, m] - times * cell[m, l]
                line[j] = line[j] - times * line[l]
                side[j] = side[j] - times * side[l]
        out = side[0] * lax.rsqrt(cell[0, 0])
        for j in range(1, 8):
            out = jnp.where(sub == j, side[j] * lax.rsqrt(cell[j, j]), out)
        done.append(out)
        for u in range(t + 1, 12):
            tail, more = rows[u], aside[u]
            old = tail
            cols = []
            for l in range(8):
                value = jnp.broadcast_to(old[:, first + l : first + l + 1], (8, 128))
                for p in range(l):
                    value = value - cols[p] * cell[l, p]
                cols.append(value * inv[l])
            for l in range(8):
                tail = tail - cols[l] * line[l]
                more = more - cols[l] * side[l]
            rows[u], aside[u] = tail, more
    return jnp.concatenate(done, axis=0)


def subspace_kernel(scale, tiles_ref, start_ref, out_ref, ghi, glo, zcat):
    def put(r, c, value):
        high, low = split(value)
        ghi[r : r + value.shape[0], c : c + value.shape[1]] = high
        glo[r : r + value.shape[0], c : c + value.shape[1]] = low

    row = lax.broadcasted_iota(jnp.int32, (128, 128), 0)
    col = lax.broadcasted_iota(jnp.int32, (128, 128), 1)
    corner = []
    for l in range(5):
        n = COUNT[l] * 8
        block = tiles_ref[BASE[l] : BASE[l] + COUNT[l]].reshape(n, 128) * scale
        diag = block[0:128]
        put(128 * l, 128 * l, jnp.where(row >= col, diag, diag.T))
        corner.append(pltpu.roll(diag[0:32], (32 + 32 * l) % 128, 1))
        if l < 4:
            rest = block[128:]
            put(128 * l + 128, 128 * l, rest)
            tall = jnp.concatenate([rest, jnp.zeros((96, 128), F32)], axis=0)
            put(128 * l, 128 * l + 128, tall.T)
    lane = lax.broadcasted_iota(jnp.int32, (32, 128), 1)
    left = corner[0]
    for l in range(1, 4):
        left = jnp.where(lane >= 32 * l, corner[l], left)
    right = jnp.where(lane < 32, corner[4], 0.0)
    put(640, 512, left)
    put(640, 640, right)
    put(512, 640, jnp.concatenate([left, jnp.zeros((96, 128), F32)], axis=0).T)
    zcat[ROWS:768] = jnp.zeros((96, 256), BF16)

    def keep(value):
        high, low = split(value)
        zcat[0:ROWS, 0:128] = high
        zcat[0:ROWS, 128:256] = low

    def times_gram():
        both = nn(ghi[...], zcat[...])
        return both[:, 0:128] + both[:, 128:256] + nn(glo[...], zcat[:, 0:128])

    def factor():
        z = zcat[0:ROWS]
        quad = dot(z, z, 0, 0)
        square = quad[0:128, 0:128] + quad[0:128, 128:256] + quad[128:256, 0:128] + quad[128:256, 128:256]
        return inverse_factor(square[0:RANK])

    def apply(high, low, inverse):
        mhi, mlo = split(jnp.concatenate([inverse, jnp.zeros((32, 128), F32)], axis=0))
        lhs = jnp.concatenate([high, low], axis=1)
        return nt(lhs, jnp.concatenate([mhi, mhi], axis=1)) + nt(high, mlo)

    keep(jnp.concatenate([start_ref[...], jnp.zeros((ROWS, 32), F32)], axis=1))
    keep(times_gram())

    def step(_, carry):
        high, low = split(times_gram())
        keep(apply(high, low, factor()))
        return carry

    lax.fori_loop(0, ITERS - 1, step, 0)
    out = apply(zcat[0:ROWS, 0:128], zcat[0:ROWS, 128:256], factor())
    out_ref[...] = out[:, 0:RANK]


def subspace(tiles, start, scale):
    return pl.pallas_call(
        functools.partial(subspace_kernel, scale),
        out_shape=jax.ShapeDtypeStruct((ROWS, RANK), F32),
        in_specs=vmem(2),
        out_specs=vmem(1)[0],
        scratch_shapes=[
            pltpu.VMEM((ROWS, 768), BF16),
            pltpu.VMEM((ROWS, 768), BF16),
            pltpu.VMEM((768, 256), BF16),
        ],
        compiler_params=pltpu.CompilerParams(vmem_limit_bytes=48 * 2**20),
        name="subspace",
    )(tiles, start)


def place():
    gx, gy, gz = lax.axis_index("gx"), lax.axis_index("gy"), lax.axis_index("gz")
    return gy, gx // 4, (gx % 4) * 2 + gz // 2, gz % 2


def device(x, y, z, core):
    return (y * 4 + z // 2, x, (z % 2) * 2 + core)


def turn(value, by, size):
    return lax.rem(value + by, size)


def greet(ids):
    barrier = pltpu.get_barrier_semaphore()
    for i in ids:
        pl.semaphore_signal(barrier, inc=1, device_id=i, device_id_type=MESH)
    return len(ids)


def remote(src, dst, send, recv, to):
    copy = pltpu.make_async_remote_copy(
        src_ref=src, dst_ref=dst, send_sem=send, recv_sem=recv, device_id=to, device_id_type=MESH
    )
    copy.start()
    return copy


def local(src, dst, sem):
    pltpu.make_async_copy(src, dst, sem).start()


def await_all(ref, sem):
    pltpu.make_async_copy(ref, ref, sem).wait()


SUM_SCRATCH = [
    pltpu.VMEM((256, 8, 128), F32),
    pltpu.VMEM((128, 8, 128), F32),
    pltpu.VMEM((128, 8, 128), F32),
    pltpu.VMEM((3, 32, 8, 128), F32),
    pltpu.VMEM((3, 8, 8, 128), F32),
    pltpu.VMEM((7, 8, 128), F32),
    pltpu.SemaphoreType.DMA((28,)),
    pltpu.SemaphoreType.DMA((28,)),
]


def sum_everywhere(out, tiles, half, first, second, third, fourth, send, recv):
    x, y, z, core = place()
    flip = core == 0
    a = jnp.where(flip, x, y)
    b = jnp.where(flip, y, x)

    def at(pa, pb, pz, pc):
        return device(jnp.where(flip, pa, pb), jnp.where(flip, pb, pa), pz, pc)

    partner = at(a, b, z, 1 - core)
    peers_a = [at(turn(a, d, 4), b, z, core) for d in range(1, 4)]
    peers_b = [at(a, turn(b, d, 4), z, core) for d in range(1, 4)]
    peers_z = [at(a, b, turn(z, d, 8), core) for d in range(1, 8)]

    def copy(src, dst, sem, to):
        return remote(src, dst, send.at[sem], recv.at[sem], to)

    def wait(copies):
        for c in copies:
            c.wait()

    mine = core * 128
    other = (1 - core) * 128
    wait([copy(tiles.at[pl.ds(other, 128)], first, 0, partner)])
    half[...] = tiles[pl.ds(mine, 128)] + first[...]
    wait([copy(half.at[pl.ds(turn(a, d, 4) * 32, 32)], second.at[d - 1], d, peers_a[d - 1]) for d in range(1, 4)])
    mine_a = a * 32
    half[pl.ds(mine_a, 32)] = half[pl.ds(mine_a, 32)] + second[0] + second[1] + second[2]
    wait([
        copy(half.at[pl.ds(mine_a + turn(b, d, 4) * 8, 8)], third.at[d - 1], 3 + d, peers_b[d - 1])
        for d in range(1, 4)
    ])
    mine_b = mine_a + b * 8
    half[pl.ds(mine_b, 8)] = half[pl.ds(mine_b, 8)] + third[0] + third[1] + third[2]
    wait([copy(half.at[mine_b + turn(z, d, 8)], fourth.at[d - 1], 6 + d, peers_z[d - 1]) for d in range(1, 8)])
    own = mine_b + z
    total = half[own]
    for d in range(7):
        total = total + fourth[d]
    out[mine + own] = total
    wait([copy(out.at[mine + own], out.at[mine + own], 13 + d, peers_z[d - 1]) for d in range(1, 8)])
    block = out.at[pl.ds(mine + mine_b, 8)]
    wait([copy(block, block, 20 + d, peers_b[d - 1]) for d in range(1, 4)])
    block = out.at[pl.ds(mine + mine_a, 32)]
    wait([copy(block, block, 23 + d, peers_a[d - 1]) for d in range(1, 4)])
    block = out.at[pl.ds(mine, 128)]
    wait([copy(block, block, 27, partner)])


def add_gram(hi, lo, tiles, fresh):
    def put(l, skip, value):
        n = value.shape[0] // 8
        at = pl.ds(BASE[l] + skip // 8, n)
        value = value.reshape(n, 8, 128)
        tiles[at] = value if fresh else tiles[at] + value

    def product(r, c, n):
        return nt(hi[r:], hi[c : c + n]) + nt(hi[r:], lo[c : c + n]) + nt(lo[r:], hi[c : c + n])

    last = product(512, 512, 160)
    lane = lax.broadcasted_iota(jnp.int32, (32, 128), 1)

    def corner(l, value):
        tail = last[128:160, 0:128]
        if l == 4:
            tail = jnp.concatenate([last[128:160, 128:160], jnp.zeros((32, 96), F32)], axis=1)
        tail = pltpu.roll(tail, (96 - 32 * (l % 4)) % 128, 1)
        put(l, 0, jnp.where(lane >= 96, tail, value[0:32]))
        put(l, 32, value[32:])

    block = product(0, 0, 256)
    corner(0, block[:, 0:128])
    corner(1, block[128:, 128:256])
    block = product(256, 256, 256)
    corner(2, block[:, 0:128])
    corner(3, block[128:, 128:256])
    corner(4, last[0:128, 0:128])


def extra_tile():
    gx, gz = lax.axis_index("gx"), lax.axis_index("gz")
    y, z = gx // 4, gx % 4
    n = 4 * z + y
    usual = n // 5 == gz
    has = jnp.logical_or(usual, jnp.logical_and(z == 0, gz == 3))
    return has, jnp.where(usual, n - 5 * gz, 1 + y)


def first_kernel(slab, out, xhi, xlo, rows, tiles, half, first, second, third, fourth, send, recv,
                 slab_send, more_send, slab_recv):
    gx, gy, gz = lax.axis_index("gx"), lax.axis_index("gy"), lax.axis_index("gz")
    x, y, z, core = place()
    ids = [(turn(gx, d, 16), gy, gz) for d in range(1, 16)]
    ids += [device(x, y, z, 1 - core)]
    ids += [device(turn(x, d, 4), y, z, core) for d in range(1, 4)]
    ids += [device(x, y, turn(z, d, 8), core) for d in (1, 3, 5, 7)]
    pl.semaphore_wait(pltpu.get_barrier_semaphore(), greet(ids))

    mine = pl.ds(gx * OWN, OWN)
    copies = []
    for d in range(1, 16):
        to = turn(gx, d, 16)
        copies.append(remote(slab.at[:, pl.ds(to * 8, 8)], rows.at[0, mine], slab_send.at[d],
                             slab_recv.at[0], (to, gy, gz)))
    local(slab.at[:, pl.ds(gx * 8, 8)], rows.at[0, mine], slab_recv.at[0])
    for e in range(5):
        n = 5 * gz + e
        to = (n % 4) * 4 + (n // 4) % 4
        src = slab.at[:, pl.ds(128 + 8 * e, 8)]

        @pl.when(to != gx)
        def _():
            remote(src, rows.at[1, mine], more_send.at[e], slab_recv.at[1], (to, gy, gz))

        @pl.when(to == gx)
        def _():
            local(src, rows.at[1, mine], slab_recv.at[1])

    def use(p):
        for j in range(8):
            high, low = split(rows[p, :, j, :])
            xhi[p, :, 128 * j : 128 * j + 128] = high
            xlo[p, :, 128 * j : 128 * j + 128] = low
        add_gram(xhi.at[p], xlo.at[p], tiles, p == 0)

    await_all(rows.at[0], slab_recv.at[0])
    use(0)
    has, _ = extra_tile()

    @pl.when(has)
    def _():
        await_all(rows.at[1], slab_recv.at[1])
        use(1)

    for c in copies:
        c.wait_send()
    for e in range(5):
        n = 5 * gz + e
        to = (n % 4) * 4 + (n // 4) % 4

        @pl.when(to != gx)
        def _():
            src = slab.at[:, pl.ds(128 + 8 * e, 8)]
            await_all(src, more_send.at[e])

    sum_everywhere(out, tiles, half, first, second, third, fourth, send, recv)


def first_gram(slab):
    return pl.pallas_call(
        first_kernel,
        out_shape=(
            jax.ShapeDtypeStruct((256, 8, 128), F32),
            jax.ShapeDtypeStruct((2, ROWS, 1024), BF16),
            jax.ShapeDtypeStruct((2, ROWS, 1024), BF16),
        ),
        in_specs=[pl.BlockSpec(memory_space=pltpu.MemorySpace.HBM)],
        out_specs=tuple(vmem(3)),
        scratch_shapes=[
            pltpu.VMEM((2, ROWS, 8, 128), F32),
            *SUM_SCRATCH,
            pltpu.SemaphoreType.DMA((16,)),
            pltpu.SemaphoreType.DMA((5,)),
            pltpu.SemaphoreType.DMA((2,)),
        ],
        compiler_params=pltpu.CompilerParams(
            collective_id=0, has_side_effects=True, vmem_limit_bytes=48 * 2**20),
        name="first_gram",
    )(slab)


def ranks(gy, core):
    low = gy < 2
    if_zero = (jnp.where(low, 2 * gy, gy + 2), jnp.where(low, 2, 1))
    if_one = (jnp.where(low, gy, 2 * gy - 2), jnp.where(low, 1, 2))
    return jnp.where(core == 0, if_zero[0], if_one[0]), jnp.where(core == 0, if_zero[1], if_one[1])


def owner(r, core):
    zero = (jnp.where(r < 4, r // 2, r - 2), jnp.where(r < 4, r % 2, 0))
    one = (jnp.where(r < 2, r, r // 2 + 1), jnp.where(r < 2, 0, r % 2))
    return jnp.where(core == 0, zero[0], one[0]), jnp.where(core == 0, zero[1], one[1])


def basis_rows(basis):
    wide = jnp.concatenate([basis, jnp.zeros((ROWS, 32), F32)], axis=1)
    high, low = split(wide.T[0:RANK])
    return jnp.concatenate([high, low], axis=0)


def contract(stacked, hi, lo):
    both = nn(stacked, hi)
    return both[0:RANK] + both[RANK:] + nn(stacked[0:RANK], lo)


def second_kernel(basis, xhi, xlo, out, qhi, qlo, part, rows, tiles, half, first, second, third, fourth,
                  send, recv, part_send, part_recv):
    gx, gy, gz = lax.axis_index("gx"), lax.axis_index("gy"), lax.axis_index("gz")
    x, y, z, core = place()
    barrier = pltpu.get_barrier_semaphore()

    def hello(i, carry):
        to = (turn(gx, i // 4, 16), turn(gy, i % 4, 4), gz)
        pl.semaphore_signal(barrier, inc=1, device_id=to, device_id_type=MESH)
        return carry

    lax.fori_loop(1, 64, hello, 0)
    ids = [device(x, y, z, 1 - core)] + [device(x, y, turn(z, d, 8), core) for d in (1, 3, 5, 7)]
    count = 63 + greet(ids)
    stacked = basis_rows(basis[...])
    has, which = extra_tile()

    def work(p):
        for j in range(0, 8, 2):
            at = pl.ds(128 * j, 256)
            value = contract(stacked, xhi[p, :, at], xlo[p, :, at])
            part[p, :, j, :] = value[:, 0:128]
            part[p, :, j + 1, :] = value[:, 128:256]

    def deal(p, tile):
        at = pl.ds(gy * 168 + tile * 8, 8)

        def one(r, carry):
            to_x = r // 6
            to_y, slot = owner(r % 6, core)
            me = jnp.logical_and(to_x == gx, to_y == gy)

            @pl.when(jnp.logical_not(me))
            def _():
                remote(part.at[p, r], rows.at[slot, at], part_send.at[p], part_recv.at[0], (to_x, to_y, gz))

            @pl.when(me)
            def _():
                local(part.at[p, r], rows.at[slot, at], part_recv.at[0])

            return carry

        lax.fori_loop(0, RANK, one, 0)

    work(0)
    pl.semaphore_wait(barrier, count)
    deal(0, gx)

    @pl.when(has)
    def _():
        work(1)
        deal(1, 16 + which)

    _, held = ranks(gy, core)

    @pl.when(held == 2)
    def _():
        await_all(rows, part_recv.at[0])
        await_all(part.at[0, pl.ds(0, 94)], part_send.at[0])

        @pl.when(has)
        def _():
            await_all(part.at[1, pl.ds(0, 94)], part_send.at[1])

        high, low = split(rows[1])
        qhi[:, 128:256] = high
        qlo[:, 128:256] = low

    @pl.when(held != 2)
    def _():
        await_all(rows.at[0], part_recv.at[0])
        await_all(part.at[0, pl.ds(0, 95)], part_send.at[0])

        @pl.when(has)
        def _():
            await_all(part.at[1, pl.ds(0, 95)], part_send.at[1])

        qhi[:, 128:256] = jnp.zeros((ROWS, 128), BF16)
        qlo[:, 128:256] = jnp.zeros((ROWS, 128), BF16)

    high, low = split(rows[0])
    qhi[:, 0:128] = high
    qlo[:, 0:128] = low
    add_gram(qhi, qlo, tiles, True)
    sum_everywhere(out, tiles, half, first, second, third, fourth, send, recv)


def second_gram(basis, xhi, xlo):
    return pl.pallas_call(
        second_kernel,
        out_shape=(
            jax.ShapeDtypeStruct((256, 8, 128), F32),
            jax.ShapeDtypeStruct((ROWS, 256), BF16),
            jax.ShapeDtypeStruct((ROWS, 256), BF16),
        ),
        in_specs=vmem(3),
        out_specs=tuple(vmem(3)),
        scratch_shapes=[
            pltpu.VMEM((2, RANK, 8, 128), F32),
            pltpu.VMEM((2, ROWS, 128), F32),
            *SUM_SCRATCH,
            pltpu.SemaphoreType.DMA((2,)),
            pltpu.SemaphoreType.DMA((1,)),
        ],
        compiler_params=pltpu.CompilerParams(
            collective_id=1, has_side_effects=True, vmem_limit_bytes=48 * 2**20),
        name="second_gram",
    )(basis, xhi, xlo)


def core_kernel(basis, qhi, qlo, out, terms, send, recv):
    gx, gy, gz = lax.axis_index("gx"), lax.axis_index("gy"), lax.axis_index("gz")
    barrier = pltpu.get_barrier_semaphore()
    count = greet([(gx, turn(gy, d, 4), gz) for d in range(1, 4)])
    value = contract(basis_rows(basis[...]), qhi[...], qlo[...])
    terms[0] = value[:, 0:128]
    terms[1] = value[:, 128:256]
    start, held = ranks(gy, gz % 2)
    pl.semaphore_wait(barrier, count)

    def deal(k):
        dst = out.at[start + k]
        for d in range(1, 4):
            to = turn(gy, d, 4)
            remote(terms.at[k, pl.ds(to * 24, 24)], dst, send.at[k, d], recv.at[0], (gx, to, gz))
        local(terms.at[k, pl.ds(gy * 24, 24)], dst, recv.at[0])

    def finish(k):
        for d in range(1, 4):
            await_all(terms.at[k, pl.ds(0, 24)], send.at[k, d])

    deal(0)

    @pl.when(held == 2)
    def _():
        deal(1)
        finish(1)

    finish(0)
    await_all(out, recv.at[0])


def core_piece(basis, qhi, qlo):
    return pl.pallas_call(
        core_kernel,
        out_shape=jax.ShapeDtypeStruct((6, 24, 128), F32),
        in_specs=vmem(3),
        out_specs=vmem(1)[0],
        scratch_shapes=[
            pltpu.VMEM((2, RANK, 128), F32),
            pltpu.SemaphoreType.DMA((2, 4)),
            pltpu.SemaphoreType.DMA((1,)),
        ],
        compiler_params=pltpu.CompilerParams(
            collective_id=2, has_side_effects=True, vmem_limit_bytes=48 * 2**20),
        name="core_piece",
    )(basis, qhi, qlo)


def body(slab, start_one, start_two):
    tiles, xhi, xlo = first_gram(slab)
    factor_one = subspace(tiles, start_one, 1.0 / (672 * 512))
    tiles, qhi, qlo = second_gram(factor_one, xhi, xlo)
    factor_two = subspace(tiles, start_two, 1.0 / (RANK * 512))
    return factor_one, factor_two, core_piece(factor_two, qhi, qlo)


def solution(mesh):
    placed = (P("gx", "gy", "gz"), P(), P())
    return jax.shard_map(
        body, mesh=mesh, in_specs=placed, out_specs=(P(), P(), P("gx", "gy", "gz")), check_vma=False
    )
```

time: 1190 us -> 294 us (0.25)
  waiting for transfers between devices: 658 us -> 0 us
  Pallas kernels: 0 us -> 282 us
  other arithmetic: 282 us -> 0 us
  blocking collectives: 120 us -> 0 us
  matrix products: 78.7 us -> 0 us
  local copies, waits for them, and re-layouts: 26.2 us -> 10.5 us
  between operations: 15 us -> 0.73 us
    psum x2 -> x0, waiting for transfers between devices: 517 us -> none  [the longest x1 260 us: body(): gram_two = lax.psum(partial_two, ('gx', 'gy', 'gz')) * scale_two]
    pallas_call x0 -> x5, Pallas kernels: none -> 282 us  [the longest x1 150 us: first_gram(): pl.pallas_call(first_kernel, out_shape=(jax.ShapeDtypeStruct((256, 8, 128...]
    another operation x80 -> x0, other arithmetic: 279 us -> none  [the longest x48 151 us: orthonormal(): factor = jnp.linalg.cholesky(square)]
    reduce_scatter x2 -> x0, waiting for transfers between devices: 140 us -> none  [the longest x1 119 us: body(): lax.psum_scatter(jnp.einsum('ir,ijc->rjc', own_first, slab, precision=pre...]
    all_to_all x2 -> x0, blocking collectives: 120 us -> none  [the longest x1 109 us: body(): lax.all_to_all(slab.reshape(row_count, col_block * depth), 'gx', split_ax...]
    dot_general x36 -> x0, matrix products: 69.7 us -> none  [the longest x16 35.5 us: subspace(): jnp.dot(gram_rows, basis, precision=precise)]
    all_to_all x6 -> x0, local copies, waits for them, and re-layouts: 13.6 us -> none  [the longest x3 12.2 us: body(): lax.all_to_all(slab.reshape(row_count, col_block * depth), 'gx', split_ax...]
  transfers between devices with their start and end apart: 4 -> 0, of which waited for: 4 -> 0; matrix products, arithmetic and copies ran while one was open for 0% -> 0% of each run, Pallas kernels for 0% -> 0%
where the time goes in v1:
time: 294 us
  Pallas kernels  282 us (96%)
  local copies, waits for them, and re-layouts  10.5 us (4%)
    pallas_call x1, Pallas kernels, first_gram(): pl.pallas_call(first_kernel, out_shape=(jax.ShapeDtypeStruct((256, 8, 128...  150 us
    pallas_call x2, Pallas kernels, subspace(): pl.pallas_call(functools.partial(subspace_kernel, scale), out_shape=jax.S...  69.3 us
    pallas_call x1, Pallas kernels, second_gram(): pl.pallas_call(second_kernel, out_shape=(jax.ShapeDtypeStruct((256, 8, 12...  59 us
    unnamed x25, local copies, waits for them, and re-layouts  10.5 us

profile of v1, /device:TPU:1, one launch (start us, length us, event | category | flops | bytes accessed | tf_op | source)
XLA Modules:
  0.0 293.7 jit_solution(7744467721126477642)
XLA Ops:
  0.6 0.0 copy-start.8
  0.6 149.6 %first_gram.1 = (f32[256,8,128]{2,1,0:T(8,128)S(1)}, bf16[2,672,1024]{2,1,0:T(8,128)(2,1)S(1)}, bf16[2,672,1024]{2,1,0:T(8,128)(2,1)}) custom-call(f32[42,168,128]{2,1,0:T(8,128)} %slab.1), custom_call_target="tpu_custom_call" | custom-call | tf_op jit(solution)/shard_map/first_gram/pallas_call | solution.py:365
  150.2 0.0 copy-start.2
  150.2 0.9 copy-done.2
  151.2 0.2 copy.6.start_ref
  151.3 0.0 copy-start.3
  151.4 1.2 copy-done.3
  152.6 34.7 %subspace.2.basis = f32[672,96]{1,0:T(8,128)S(1)} custom-call(f32[256,8,128]{2,1,0:T(8,128)S(1)} %copy-done.3, f32[672,96]{1,0:T(8,128)S(1)} %copy.6.start_ref), custom_call_target="tpu_custom_call" | custom-call | tf_op jit(solution)/shard_map/subspace/pallas_call | solution.py:153
  187.3 0.0 copy-start.9
  187.3 59.0 %second_gram.1 = (f32[256,8,128]{2,1,0:T(8,128)S(1)}, bf16[672,256]{1,0:T(8,128)(2,1)S(1)}, bf16[672,256]{1,0:T(8,128)(2,1)S(1)}) custom-call(f32[672,96]{1,0:T(8,128)S(1)} %subspace.2.basis, bf16[2,672,1024]{2,1,0:T(8,128)(2,1)S(1)} %get-tuple-element.10.xhi, bf16[2,672,1024]{2,1,0:T(8,128)(2,1)} %get-tuple-element.11.xlo), custom_call_target="tpu_custom_call" | custom-call | tf_op jit(solution)/shard_map/second_gram/pallas_call | solution.py:499
  246.3 0.0 copy-start
  246.3 1.0 copy-done
  247.2 0.7 copy-done.4
  248.0 0.7 copy-done.6
  248.7 0.2 copy.7.start_ref
  248.9 0.0 copy-start.1
  248.9 1.2 copy-done.1
  250.1 34.7 %subspace.3.basis = f32[672,96]{1,0:T(8,128)S(1)} custom-call(f32[256,8,128]{2,1,0:T(8,128)S(1)} %copy-done.1, f32[672,96]{1,0:T(8,128)S(1)} %copy.7.start_ref), custom_call_target="tpu_custom_call" | custom-call | tf_op jit(solution)/shard_map/subspace/pallas_call | solution.py:153
  284.8 1.0 copy-done.5
  285.8 1.0 copy-done.7
  286.7 4.6 %core_piece.1 = f32[6,24,128]{2,1,0:T(8,128)S(1)} custom-call(f32[672,96]{1,0:T(8,128)S(1)} %subspace.3.basis, bf16[672,256]{1,0:T(8,128)(2,1)S(1)} %copy-done.5, bf16[672,256]{1,0:T(8,128)(2,1)S(1)} %copy-done.7), custom_call_target="tpu_custom_call" | custom-call | tf_op jit(solution)/shard_map/core_piece/pallas_call | solution.py:554
  291.3 0.9 copy.9
  292.2 0.9 copy.8
  293.1 0.6 copy.11
  (6 shorter events, 0.0 us)
Async XLA Ops:
  0.6 150.6 %copy-start.8 = (f32[672,96]{0,1:T(8,128)S(1)}, f32[672,96]{0,1:T(8,128)}, u32[]{:S(2)}) copy-start(f32[672,96]{0,1:T(8,128)} %param.4) | copy-start | bytes 774148
  150.2 1.0 copy-start.2
  151.3 1.2 copy-start.3
  187.3 61.5 %copy-start.9 = (f32[672,96]{0,1:T(8,128)S(1)}, f32[672,96]{0,1:T(8,128)}, u32[]{:S(2)}) copy-start(f32[672,96]{0,1:T(8,128)} %param.5) | copy-start | bytes 774148
  246.3 1.0 copy-start
  247.2 0.8 copy-start.4
  248.0 0.7 copy-start.6
  248.9 1.2 copy-start.1
  284.8 1.0 copy-start.5
  285.8 1.0 copy-start.7

commit v2 on v1

--- a/solution.py
+++ b/solution.py
@@ -46,39 +46,44 @@
     sub = lax.broadcasted_iota(jnp.int32, (8, 128), 0)
     aside = [(lane == sub + 8 * t).astype(F32) for t in range(12)]
     done = []
+    ahead = [jnp.broadcast_to(rows[0][:, l : l + 1], (8, 128)) for l in range(8)]
     for t in range(12):
         first = 8 * t
         tile, extra = rows[t], aside[t]
-        cell = {
-            (j, l): jnp.broadcast_to(tile[j : j + 1, first + l : first + l + 1], (8, 128))
-            for j in range(8)
-            for l in range(j + 1)
-        }
-        line = [jnp.broadcast_to(tile[j : j + 1, :], (8, 128)) for j in range(8)]
-        side = [jnp.broadcast_to(extra[j : j + 1, :], (8, 128)) for j in range(8)]
-        inv = []
+        wide = ahead
+        cell, line, side, inv = {}, [], [], []
+        pivots = None
         for l in range(8):
-            flip = 1.0 / cell[l, l]
-            inv.append(flip)
-            for j in range(l + 1, 8):
-                times = cell[j, l] * flip
-                for m in range(l + 1, j + 1):
-                    cell[j, m] = cell[j, m] - times * cell[m, l]
-                line[j] = line[j] - times * line[l]
-                side[j] = side[j] - times * side[l]
-        out = side[0] * lax.rsqrt(cell[0, 0])
-        for j in range(1, 8):
-            out = jnp.where(sub == j, side[j] * lax.rsqrt(cell[j, j]), out)
+            for m in range(l, 8):
+                cell[m, l] = jnp.broadcast_to(wide[m][l : l + 1, :], (8, 128))
+            line.append(jnp.broadcast_to(tile[l : l + 1, :], (8, 128)))
+            side.append(jnp.broadcast_to(extra[l : l + 1, :], (8, 128)))
+            inv.append(1.0 / cell[l, l])
+            pivots = cell[l, l] if l == 0 else jnp.where(sub == l, cell[l, l], pivots)
+            if l < 7:
+                times = jnp.where(sub > l, wide[l] * inv[l], 0.0)
+                for m in range(l + 1, 8):
+                    wide[m] = wide[m] - times * cell[m, l]
+                tile = tile - times * line[l]
+                extra = extra - times * side[l]
+        out = extra * lax.rsqrt(pivots)
         done.append(out)
         for u in range(t + 1, 12):
             tail, more = rows[u], aside[u]
-            old = tail
-            cols = []
+            raw, cols = [], []
             for l in range(8):
-                value = jnp.broadcast_to(old[:, first + l : first + l + 1], (8, 128))
+                value = jnp.broadcast_to(tail[:, first + l : first + l + 1], (8, 128))
                 for p in range(l):
                     value = value - cols[p] * cell[l, p]
+                raw.append(value)
                 cols.append(value * inv[l])
+            if u == t + 1:
+                ahead = []
+                for m in range(8):
+                    value = jnp.broadcast_to(tail[:, first + 8 + m : first + 9 + m], (8, 128))
+                    for l in range(8):
+                        value = value - cols[l] * jnp.broadcast_to(raw[l][m : m + 1, :], (8, 128))
+                    ahead.append(value)
             for l in range(8):
                 tail = tail - cols[l] * line[l]
                 more = more - cols[l] * side[l]
@@ -208,8 +213,8 @@
     pltpu.VMEM((3, 32, 8, 128), F32),
     pltpu.VMEM((3, 8, 8, 128), F32),
     pltpu.VMEM((7, 8, 128), F32),
-    pltpu.SemaphoreType.DMA((28,)),
-    pltpu.SemaphoreType.DMA((28,)),
+    pltpu.SemaphoreType.DMA((76,)),
+    pltpu.SemaphoreType.DMA((76,)),
 ]
 
 
@@ -226,40 +231,74 @@
     peers_a = [at(turn(a, d, 4), b, z, core) for d in range(1, 4)]
     peers_b = [at(a, turn(b, d, 4), z, core) for d in range(1, 4)]
     peers_z = [at(a, b, turn(z, d, 8), core) for d in range(1, 8)]
-
-    def copy(src, dst, sem, to):
-        return remote(src, dst, send.at[sem], recv.at[sem], to)
-
-    def wait(copies):
-        for c in copies:
-            c.wait()
-
     mine = core * 128
     other = (1 - core) * 128
-    wait([copy(tiles.at[pl.ds(other, 128)], first, 0, partner)])
-    half[...] = tiles[pl.ds(mine, 128)] + first[...]
-    wait([copy(half.at[pl.ds(turn(a, d, 4) * 32, 32)], second.at[d - 1], d, peers_a[d - 1]) for d in range(1, 4)])
-    mine_a = a * 32
-    half[pl.ds(mine_a, 32)] = half[pl.ds(mine_a, 32)] + second[0] + second[1] + second[2]
-    wait([
-        copy(half.at[pl.ds(mine_a + turn(b, d, 4) * 8, 8)], third.at[d - 1], 3 + d, peers_b[d - 1])
-        for d in range(1, 4)
-    ])
-    mine_b = mine_a + b * 8
-    half[pl.ds(mine_b, 8)] = half[pl.ds(mine_b, 8)] + third[0] + third[1] + third[2]
-    wait([copy(half.at[mine_b + turn(z, d, 8)], fourth.at[d - 1], 6 + d, peers_z[d - 1]) for d in range(1, 8)])
-    own = mine_b + z
-    total = half[own]
+    copies = []
+
+    def copy(src, dst, sem, to):
+        copies.append(remote(src, dst, send.at[sem], recv.at[sem], to))
+        return copies[-1]
+
+    def piece(pa, pb):
+        return pa * 32 + pb * 8
+
+    order = (1, 2, 3, 0)
+    paired, across = {}, {}
+    for e in order:
+        for d in order:
+            p = piece(turn(b, d, 4), turn(a, e, 4))
+            paired[d, e] = copy(tiles.at[pl.ds(other + p, 8)], first.at[pl.ds(p, 8)], 4 * d + e, partner)
+    for e in order:
+        for d in order:
+            paired[d, e].wait_recv()
+            p = pl.ds(piece(turn(a, d, 4), turn(b, e, 4)), 8)
+            half[p] = tiles[pl.ds(mine + piece(turn(a, d, 4), turn(b, e, 4)), 8)] + first[p]
+            if d:
+                across[d, e] = copy(half.at[p], second.at[d - 1, pl.ds(turn(b, e, 4) * 8, 8)],
+                                    12 + 4 * d + e, peers_a[d - 1])
+    along = []
+    for e in order:
+        for d in range(1, 4):
+            across[d, e].wait_recv()
+        p = pl.ds(piece(a, turn(b, e, 4)), 8)
+        q = pl.ds(turn(b, e, 4) * 8, 8)
+        half[p] = half[p] + second[0, q] + second[1, q] + second[2, q]
+        if e:
+            along.append(copy(half.at[p], third.at[e - 1], 27 + e, peers_b[e - 1]))
+    for c in along:
+        c.wait_recv()
+    home = piece(a, b)
+    p = pl.ds(home, 8)
+    half[p] = half[p] + third[0] + third[1] + third[2]
+    for c in [copy(half.at[home + turn(z, d, 8)], fourth.at[d - 1], 30 + d, peers_z[d - 1]) for d in range(1, 8)]:
+        c.wait_recv()
+    total = half[home + z]
     for d in range(7):
         total = total + fourth[d]
-    out[mine + own] = total
-    wait([copy(out.at[mine + own], out.at[mine + own], 13 + d, peers_z[d - 1]) for d in range(1, 8)])
-    block = out.at[pl.ds(mine + mine_b, 8)]
-    wait([copy(block, block, 20 + d, peers_b[d - 1]) for d in range(1, 4)])
-    block = out.at[pl.ds(mine + mine_a, 32)]
-    wait([copy(block, block, 23 + d, peers_a[d - 1]) for d in range(1, 4)])
-    block = out.at[pl.ds(mine, 128)]
-    wait([copy(block, block, 27, partner)])
+    own = mine + home + z
+    out[own] = total
+    for c in [copy(out.at[own], out.at[own], 37 + d, peers_z[d - 1]) for d in range(1, 8)]:
+        c.wait_recv()
+
+    def block(d, e):
+        return out.at[pl.ds(mine + piece(turn(a, 4 - d, 4), turn(b, 4 - e, 4)), 8)]
+
+    along = [copy(block(0, 0), block(0, 0), 44 + e, peers_b[e - 1]) for e in range(1, 4)]
+    across, paired = {}, []
+    for e in range(4):
+        if e:
+            along[e - 1].wait_recv()
+        for d in range(1, 4):
+            across[d, e] = copy(block(0, e), block(0, e), 44 + 4 * d + e, peers_a[d - 1])
+        paired.append(copy(block(0, e), block(0, e), 60 + e, partner))
+    for e in range(4):
+        for d in range(1, 4):
+            across[d, e].wait_recv()
+            paired.append(copy(block(d, e), block(d, e), 60 + 4 * d + e, partner))
+    for c in paired:
+        c.wait_recv()
+    for c in copies:
+        c.wait_send()
 
 
 def add_gram(hi, lo, tiles, fresh):
@@ -292,13 +331,19 @@
     corner(4, last[0:128, 0:128])
 
 
+def extra_owner(gz, e):
+    n = 5 * gz + e
+    return ((n // 4 + n) % 4) * 4 + n % 4
+
+
 def extra_tile():
     gx, gz = lax.axis_index("gx"), lax.axis_index("gz")
-    y, z = gx // 4, gx % 4
-    n = 4 * z + y
-    usual = n // 5 == gz
-    has = jnp.logical_or(usual, jnp.logical_and(z == 0, gz == 3))
-    return has, jnp.where(usual, n - 5 * gz, 1 + y)
+    has, which = False, 0
+    for e in range(5):
+        taken = extra_owner(gz, e) == gx
+        has = jnp.logical_or(has, taken)
+        which = jnp.where(taken, e, which)
+    return has, which
 
 
 def first_kernel(slab, out, xhi, xlo, rows, tiles, half, first, second, third, fourth, send, recv,
@@ -312,34 +357,34 @@
     pl.semaphore_wait(pltpu.get_barrier_semaphore(), greet(ids))
 
     mine = pl.ds(gx * OWN, OWN)
+    for e in range(5):
+        to = extra_owner(gz, e)
+        src = slab.at[:, pl.ds(128 + 8 * e, 8)]
+
+        @pl.when(to != gx)
+        def _():
+            remote(src, rows.at[1, mine], more_send.at[e], slab_recv.at[1], (to, gy, gz))
+
+        @pl.when(to == gx)
+        def _():
+            local(src, rows.at[1, mine], slab_recv.at[1])
+
     copies = []
     for d in range(1, 16):
         to = turn(gx, d, 16)
         copies.append(remote(slab.at[:, pl.ds(to * 8, 8)], rows.at[0, mine], slab_send.at[d],
                              slab_recv.at[0], (to, gy, gz)))
     local(slab.at[:, pl.ds(gx * 8, 8)], rows.at[0, mine], slab_recv.at[0])
-    for e in range(5):
-        n = 5 * gz + e
-        to = (n % 4) * 4 + (n // 4) % 4
-        src = slab.at[:, pl.ds(128 + 8 * e, 8)]
-
-        @pl.when(to != gx)
-        def _():
-            remote(src, rows.at[1, mine], more_send.at[e], slab_recv.at[1], (to, gy, gz))
-
-        @pl.when(to == gx)
-        def _():
-            local(src, rows.at[1, mine], slab_recv.at[1])
+
+    tiles[...] = jnp.zeros_like(tiles)
 
     def use(p):
         for j in range(8):
             high, low = split(rows[p, :, j, :])
             xhi[p, :, 128 * j : 128 * j + 128] = high
             xlo[p, :, 128 * j : 128 * j + 128] = low
-        add_gram(xhi.at[p], xlo.at[p], tiles, p == 0)
-
-    await_all(rows.at[0], slab_recv.at[0])
-    use(0)
+        add_gram(xhi.at[p], xlo.at[p], tiles, False)
+
     has, _ = extra_tile()
 
     @pl.when(has)
@@ -347,11 +392,13 @@
         await_all(rows.at[1], slab_recv.at[1])
         use(1)
 
+    await_all(rows.at[0], slab_recv.at[0])
+    use(0)
+
     for c in copies:
         c.wait_send()
     for e in range(5):
-        n = 5 * gz + e
-        to = (n % 4) * 4 + (n // 4) % 4
+        to = extra_owner(gz, e)
 
         @pl.when(to != gx)
         def _():
@@ -435,9 +482,10 @@
     def deal(p, tile):
         at = pl.ds(gy * 168 + tile * 8, 8)
 
-        def one(r, carry):
-            to_x = r // 6
-            to_y, slot = owner(r % 6, core)
+        def one(i, carry):
+            to_x = turn(gx, i // 6, 16)
+            to_y, slot = owner(i % 6, core)
+            r = to_x * 6 + i % 6
             me = jnp.logical_and(to_x == gx, to_y == gy)
 
             @pl.when(jnp.logical_not(me))

time: 294 us -> 263 us (0.89)
  Pallas kernels: 282 us -> 251 us
    pallas_call x2, Pallas kernels: 69.3 us -> 53.8 us  [subspace(): pl.pallas_call(functools.partial(subspace_kernel, scale), out_shape=jax.S...]
    pallas_call x1, Pallas kernels: 150 us -> 137 us  [first_gram(): pl.pallas_call(first_kernel, out_shape=(jax.ShapeDtypeStruct((256, 8, 128...]
where the time goes in v2:
time: 263 us
  Pallas kernels  251 us (95%)
  local copies, waits for them, and re-layouts  10.5 us (4%)
    pallas_call x1, Pallas kernels, first_gram(): pl.pallas_call(first_kernel, out_shape=(jax.ShapeDtypeStruct((256, 8, 128...  137 us
    pallas_call x1, Pallas kernels, second_gram(): pl.pallas_call(second_kernel, out_shape=(jax.ShapeDtypeStruct((256, 8, 12...  56.3 us
    pallas_call x2, Pallas kernels, subspace(): pl.pallas_call(functools.partial(subspace_kernel, scale), out_shape=jax.S...  53.8 us
    unnamed x25, local copies, waits for them, and re-layouts  10.5 us

profile of v2, /device:TPU:1, one launch (start us, length us, event | category | flops | bytes accessed | tf_op | source)
XLA Modules:
  0.0 262.5 jit_solution(13912596537331998466)
XLA Ops:
  0.6 0.0 copy-start.8
  0.6 136.6 %first_gram.1 = (f32[256,8,128]{2,1,0:T(8,128)S(1)}, bf16[2,672,1024]{2,1,0:T(8,128)(2,1)S(1)}, bf16[2,672,1024]{2,1,0:T(8,128)(2,1)}) custom-call(f32[42,168,128]{2,1,0:T(8,128)} %slab.1), custom_call_target="tpu_custom_call" | custom-call | tf_op jit(solution)/shard_map/first_gram/pallas_call | solution.py:412
  137.3 0.0 copy-start.2
  137.3 0.9 copy-done.2
  138.2 0.0 copy-done.8
  138.2 0.2 copy.6.start_ref
  138.4 0.0 copy-start.3
  138.4 1.2 copy-done.3
  139.6 26.9 %subspace.2.basis = f32[672,96]{1,0:T(8,128)S(1)} custom-call(f32[256,8,128]{2,1,0:T(8,128)S(1)} %copy-done.3, f32[672,96]{1,0:T(8,128)S(1)} %copy.6.start_ref), custom_call_target="tpu_custom_call" | custom-call | tf_op jit(solution)/shard_map/subspace/pallas_call | solution.py:158
  166.5 0.0 copy-start.9
  166.5 56.3 %second_gram.1 = (f32[256,8,128]{2,1,0:T(8,128)S(1)}, bf16[672,256]{1,0:T(8,128)(2,1)S(1)}, bf16[672,256]{1,0:T(8,128)(2,1)S(1)}) custom-call(f32[672,96]{1,0:T(8,128)S(1)} %subspace.2.basis, bf16[2,672,1024]{2,1,0:T(8,128)(2,1)S(1)} %get-tuple-element.10.xhi, bf16[2,672,1024]{2,1,0:T(8,128)(2,1)} %get-tuple-element.11.xlo), custom_call_target="tpu_custom_call" | custom-call | tf_op jit(solution)/shard_map/second_gram/pallas_call | solution.py:547
  222.8 0.0 copy-start
  222.8 1.0 copy-done
  223.8 0.7 copy-done.4
  224.5 0.7 copy-done.6
  225.2 0.2 copy.7.start_ref
  225.4 1.2 copy-done.1
  226.6 26.9 %subspace.3.basis = f32[672,96]{1,0:T(8,128)S(1)} custom-call(f32[256,8,128]{2,1,0:T(8,128)S(1)} %copy-done.1, f32[672,96]{1,0:T(8,128)S(1)} %copy.7.start_ref), custom_call_target="tpu_custom_call" | custom-call | tf_op jit(solution)/shard_map/subspace/pallas_call | solution.py:158
  253.5 1.0 copy-done.5
  254.5 1.0 copy-done.7
  255.5 4.6 %core_piece.1 = f32[6,24,128]{2,1,0:T(8,128)S(1)} custom-call(f32[672,96]{1,0:T(8,128)S(1)} %subspace.3.basis, bf16[672,256]{1,0:T(8,128)(2,1)S(1)} %copy-done.5, bf16[672,256]{1,0:T(8,128)(2,1)S(1)} %copy-done.7), custom_call_target="tpu_custom_call" | custom-call | tf_op jit(solution)/shard_map/core_piece/pallas_call | solution.py:602
  260.1 0.9 copy.9
  261.0 0.9 copy.8
  261.9 0.6 copy.11
  (6 shorter events, 0.0 us)
Async XLA Ops:
  0.6 137.6 %copy-start.8 = (f32[672,96]{0,1:T(8,128)S(1)}, f32[672,96]{0,1:T(8,128)}, u32[]{:S(2)}) copy-start(f32[672,96]{0,1:T(8,128)} %param.4) | copy-start | bytes 774148
  137.3 1.0 copy-start.2
  138.4 1.2 copy-start.3
  166.5 58.7 %copy-start.9 = (f32[672,96]{0,1:T(8,128)S(1)}, f32[672,96]{0,1:T(8,128)}, u32[]{:S(2)}) copy-start(f32[672,96]{0,1:T(8,128)} %param.5) | copy-start | bytes 774148
  222.8 1.0 copy-start
  223.8 0.8 copy-start.4
  224.5 0.7 copy-start.6
  225.4 1.2 copy-start.1
  253.5 1.0 copy-start.5
  254.5 1.0 copy-start.7

commit v3 on v2

--- a/solution.py
+++ b/solution.py
@@ -91,7 +91,7 @@
     return jnp.concatenate(done, axis=0)
 
 
-def subspace_kernel(scale, tiles_ref, start_ref, out_ref, ghi, glo, zcat):
+def subspace(scale, tiles_ref, start_ref, out_ref, ghi, glo, zcat):
     def put(r, c, value):
         high, low = split(value)
         ghi[r : r + value.shape[0], c : c + value.shape[1]] = high
@@ -152,22 +152,6 @@
     lax.fori_loop(0, ITERS - 1, step, 0)
     out = apply(zcat[0:ROWS, 0:128], zcat[0:ROWS, 128:256], factor())
     out_ref[...] = out[:, 0:RANK]
-
-
-def subspace(tiles, start, scale):
-    return pl.pallas_call(
-        functools.partial(subspace_kernel, scale),
-        out_shape=jax.ShapeDtypeStruct((ROWS, RANK), F32),
-        in_specs=vmem(2),
-        out_specs=vmem(1)[0],
-        scratch_shapes=[
-            pltpu.VMEM((ROWS, 768), BF16),
-            pltpu.VMEM((ROWS, 768), BF16),
-            pltpu.VMEM((768, 256), BF16),
-        ],
-        compiler_params=pltpu.CompilerParams(vmem_limit_bytes=48 * 2**20),
-        name="subspace",
-    )(tiles, start)
 
 
 def place():
@@ -346,16 +330,8 @@
     return has, which
 
 
-def first_kernel(slab, out, xhi, xlo, rows, tiles, half, first, second, third, fourth, send, recv,
-                 slab_send, more_send, slab_recv):
+def first_gram(slab, xhi, xlo, rows, tiles, slab_send, more_send, slab_recv):
     gx, gy, gz = lax.axis_index("gx"), lax.axis_index("gy"), lax.axis_index("gz")
-    x, y, z, core = place()
-    ids = [(turn(gx, d, 16), gy, gz) for d in range(1, 16)]
-    ids += [device(x, y, z, 1 - core)]
-    ids += [device(turn(x, d, 4), y, z, core) for d in range(1, 4)]
-    ids += [device(x, y, turn(z, d, 8), core) for d in (1, 3, 5, 7)]
-    pl.semaphore_wait(pltpu.get_barrier_semaphore(), greet(ids))
-
     mine = pl.ds(gx * OWN, OWN)
     for e in range(5):
         to = extra_owner(gz, e)
@@ -405,31 +381,6 @@
             src = slab.at[:, pl.ds(128 + 8 * e, 8)]
             await_all(src, more_send.at[e])
 
-    sum_everywhere(out, tiles, half, first, second, third, fourth, send, recv)
-
-
-def first_gram(slab):
-    return pl.pallas_call(
-        first_kernel,
-        out_shape=(
-            jax.ShapeDtypeStruct((256, 8, 128), F32),
-            jax.ShapeDtypeStruct((2, ROWS, 1024), BF16),
-            jax.ShapeDtypeStruct((2, ROWS, 1024), BF16),
-        ),
-        in_specs=[pl.BlockSpec(memory_space=pltpu.MemorySpace.HBM)],
-        out_specs=tuple(vmem(3)),
-        scratch_shapes=[
-            pltpu.VMEM((2, ROWS, 8, 128), F32),
-            *SUM_SCRATCH,
-            pltpu.SemaphoreType.DMA((16,)),
-            pltpu.SemaphoreType.DMA((5,)),
-            pltpu.SemaphoreType.DMA((2,)),
-        ],
-        compiler_params=pltpu.CompilerParams(
-            collective_id=0, has_side_effects=True, vmem_limit_bytes=48 * 2**20),
-        name="first_gram",
-    )(slab)
-
 
 def ranks(gy, core):
     low = gy < 2
@@ -455,20 +406,9 @@
     return both[0:RANK] + both[RANK:] + nn(stacked[0:RANK], lo)
 
 
-def second_kernel(basis, xhi, xlo, out, qhi, qlo, part, rows, tiles, half, first, second, third, fourth,
-                  send, recv, part_send, part_recv):
+def second_gram(basis, xhi, xlo, qhi, qlo, part, rows, tiles, part_send, part_recv):
     gx, gy, gz = lax.axis_index("gx"), lax.axis_index("gy"), lax.axis_index("gz")
-    x, y, z, core = place()
-    barrier = pltpu.get_barrier_semaphore()
-
-    def hello(i, carry):
-        to = (turn(gx, i // 4, 16), turn(gy, i % 4, 4), gz)
-        pl.semaphore_signal(barrier, inc=1, device_id=to, device_id_type=MESH)
-        return carry
-
-    lax.fori_loop(1, 64, hello, 0)
-    ids = [device(x, y, z, 1 - core)] + [device(x, y, turn(z, d, 8), core) for d in (1, 3, 5, 7)]
-    count = 63 + greet(ids)
+    core = gz % 2
     stacked = basis_rows(basis[...])
     has, which = extra_tile()
 
@@ -501,7 +441,6 @@
         lax.fori_loop(0, RANK, one, 0)
 
     work(0)
-    pl.semaphore_wait(barrier, count)
     deal(0, gx)
 
     @pl.when(has)
@@ -540,41 +479,14 @@
     qhi[:, 0:128] = high
     qlo[:, 0:128] = low
     add_gram(qhi, qlo, tiles, True)
-    sum_everywhere(out, tiles, half, first, second, third, fourth, send, recv)
-
-
-def second_gram(basis, xhi, xlo):
-    return pl.pallas_call(
-        second_kernel,
-        out_shape=(
-            jax.ShapeDtypeStruct((256, 8, 128), F32),
-            jax.ShapeDtypeStruct((ROWS, 256), BF16),
-            jax.ShapeDtypeStruct((ROWS, 256), BF16),
-        ),
-        in_specs=vmem(3),
-        out_specs=tuple(vmem(3)),
-        scratch_shapes=[
-            pltpu.VMEM((2, RANK, 8, 128), F32),
-            pltpu.VMEM((2, ROWS, 128), F32),
-            *SUM_SCRATCH,
-            pltpu.SemaphoreType.DMA((2,)),
-            pltpu.SemaphoreType.DMA((1,)),
-        ],
-        compiler_params=pltpu.CompilerParams(
-            collective_id=1, has_side_effects=True, vmem_limit_bytes=48 * 2**20),
-        name="second_gram",
-    )(basis, xhi, xlo)
-
-
-def core_kernel(basis, qhi, qlo, out, terms, send, recv):
+
+
+def core_piece(basis, qhi, qlo, out, terms, send, recv):
     gx, gy, gz = lax.axis_index("gx"), lax.axis_index("gy"), lax.axis_index("gz")
-    barrier = pltpu.get_barrier_semaphore()
-    count = greet([(gx, turn(gy, d, 4), gz) for d in range(1, 4)])
     value = contract(basis_rows(basis[...]), qhi[...], qlo[...])
     terms[0] = value[:, 0:128]
     terms[1] = value[:, 128:256]
     start, held = ranks(gy, gz % 2)
-    pl.semaphore_wait(barrier, count)
 
     def deal(k):
         dst = out.at[start + k]
@@ -598,29 +510,72 @@
     await_all(out, recv.at[0])
 
 
-def core_piece(basis, qhi, qlo):
+def arrive():
+    gx, gy, gz = lax.axis_index("gx"), lax.axis_index("gy"), lax.axis_index("gz")
+    x, y, z, core = place()
+    barrier = pltpu.get_barrier_semaphore()
+
+    def hello(i, carry):
+        to = (turn(gx, i // 4, 16), turn(gy, i % 4, 4), gz)
+        pl.semaphore_signal(barrier, inc=1, device_id=to, device_id_type=MESH)
+        return carry
+
+    lax.fori_loop(1, 64, hello, 0)
+    ids = [device(x, y, z, 1 - core)] + [device(x, y, turn(z, d, 8), core) for d in (1, 3, 5, 7)]
+    pl.semaphore_wait(barrier, 63 + greet(ids))
+
+
+def kernel(slab, start_one, start_two, factor_one, factor_two, core, xhi, xlo, columns, sums, part, rows, qhi, qlo,
+           ghi, glo, zcat, terms, slab_send, more_send, slab_recv, part_send, part_recv, core_send, core_recv, *sum_refs):
+    one, two = sum_refs[: len(SUM_SCRATCH)], sum_refs[len(SUM_SCRATCH) :]
+    arrive()
+    first_gram(slab, xhi, xlo, columns, one[0], slab_send, more_send, slab_recv)
+    sum_everywhere(sums.at[0], *one)
+    subspace(1.0 / (ROWS * 512), sums.at[0], start_one, factor_one, ghi, glo, zcat)
+    second_gram(factor_one, xhi, xlo, qhi, qlo, part, rows, two[0], part_send, part_recv)
+    sum_everywhere(sums.at[1], *two)
+    subspace(1.0 / (RANK * 512), sums.at[1], start_two, factor_two, ghi, glo, zcat)
+    core_piece(factor_two, qhi, qlo, core, terms, core_send, core_recv)
+
+
+def body(slab, start_one, start_two):
+    dma = pltpu.SemaphoreType.DMA
     return pl.pallas_call(
-        core_kernel,
-        out_shape=jax.ShapeDtypeStruct((6, 24, 128), F32),
-        in_specs=vmem(3),
-        out_specs=vmem(1)[0],
+        kernel,
+        out_shape=(
+            jax.ShapeDtypeStruct((ROWS, RANK), F32),
+            jax.ShapeDtypeStruct((ROWS, RANK), F32),
+            jax.ShapeDtypeStruct((6, 24, 128), F32),
+        ),
+        in_specs=[pl.BlockSpec(memory_space=pltpu.MemorySpace.HBM), *vmem(2)],
+        out_specs=tuple(vmem(3)),
         scratch_shapes=[
+            pltpu.VMEM((2, ROWS, 1024), BF16),
+            pltpu.VMEM((2, ROWS, 1024), BF16),
+            pltpu.VMEM((2, ROWS, 8, 128), F32),
+            pltpu.VMEM((2, 256, 8, 128), F32),
+            pltpu.VMEM((2, RANK, 8, 128), F32),
+            pltpu.VMEM((2, ROWS, 128), F32),
+            pltpu.VMEM((ROWS, 256), BF16),
+            pltpu.VMEM((ROWS, 256), BF16),
+            pltpu.VMEM((ROWS, 768), BF16),
+            pltpu.VMEM((ROWS, 768), BF16),
+            pltpu.VMEM((768, 256), BF16),
             pltpu.VMEM((2, RANK, 128), F32),
-            pltpu.SemaphoreType.DMA((2, 4)),
-            pltpu.SemaphoreType.DMA((1,)),
+            dma((16,)),
+            dma((5,)),
+            dma((2,)),
+            dma((2,)),
+            dma((1,)),
+            dma((2, 4)),
+            dma((1,)),
+            *SUM_SCRATCH,
+            *SUM_SCRATCH,
         ],
         compiler_params=pltpu.CompilerParams(
-            collective_id=2, has_side_effects=True, vmem_limit_bytes=48 * 2**20),
-        name="core_piece",
-    )(basis, qhi, qlo)
-
-
-def body(slab, start_one, start_two):
-    tiles, xhi, xlo = first_gram(slab)
-    factor_one = subspace(tiles, start_one, 1.0 / (672 * 512))
-    tiles, qhi, qlo = second_gram(factor_one, xhi, xlo)
-    factor_two = subspace(tiles, start_two, 1.0 / (RANK * 512))
-    return factor_one, factor_two, core_piece(factor_two, qhi, qlo)
+            collective_id=0, has_side_effects=True, vmem_limit_bytes=48 * 2**20),
+        name="hosvd",
+    )(slab, start_one, start_two)
 
 
 def solution(mesh):

time: 263 us -> 252 us (0.958)
  Pallas kernels: 251 us -> 245 us
  local copies, waits for them, and re-layouts: 10.5 us -> 6.66 us
    pallas_call x5 -> x1, Pallas kernels: 251 us -> 245 us  [body(): pl.pallas_call(kernel, out_shape=(jax.ShapeDtypeStruct((ROWS, RANK), F32)...]
    unnamed x25 -> x5, local copies, waits for them, and re-layouts: 10.5 us -> 4.91 us
where the time goes in v3:
time: 252 us
  Pallas kernels  245 us (97%)
  local copies, waits for them, and re-layouts  6.66 us (3%)
    pallas_call x1, Pallas kernels, body(): pl.pallas_call(kernel, out_shape=(jax.ShapeDtypeStruct((ROWS, RANK), F32)...  245 us

profile of v3, /device:TPU:1, one launch (start us, length us, event | category | flops | bytes accessed | tf_op | source)
XLA Modules:
  0.0 251.9 jit_solution(13220207638873309192)
XLA Ops:
  0.6 1.1 copy.6.start_one
  1.8 1.1 copy.7.start_two
  2.9 0.0 copy-start
  2.9 2.0 copy-done
  4.9 244.6 %hosvd.1 = (f32[672,96]{1,0:T(8,128)S(1)}, f32[672,96]{1,0:T(8,128)S(1)}, f32[6,24,128]{2,1,0:T(8,128)S(1)}) custom-call(f32[42,168,128]{2,1,0:T(8,128)S(1)} %copy-done, f32[672,96]{1,0:T(8,128)S(1)} %copy.6.start_one, f32[672,96]{1,0:T(8,128)S(1)} %copy.7.start_two), custom_call_target="tpu_custom_call" | custom-call | tf_op jit(solution)/shard_map/hosvd/pallas_call | solution.py:543
  249.5 0.9 copy.8
  250.4 0.9 copy.9
  251.3 0.6 copy.11
Async XLA Ops:
  2.9 2.0 copy-start

commit v4 on v3

--- a/solution.py
+++ b/solution.py
@@ -68,26 +68,49 @@
                 extra = extra - times * side[l]
         out = extra * lax.rsqrt(pivots)
         done.append(out)
-        for u in range(t + 1, 12):
+        if t + 3 < 12:
+            high, low = split(tile * lax.rsqrt(pivots))
+            high_side, low_side = split(extra * lax.rsqrt(pivots))
+            left = jnp.concatenate([high, high, low, jnp.zeros_like(low)], axis=0)
+            right = jnp.concatenate([high, low, high, jnp.zeros_like(low)], axis=0)
+            more = jnp.concatenate([high_side, low_side, high_side, jnp.zeros_like(low)], axis=0)
+            change = dot(left, jnp.concatenate([right, more], axis=1), 0, 0)
+            for u in range(t + 3, 12):
+                rows[u] = rows[u] - change[8 * u : 8 * u + 8, 0:128]
+                aside[u] = aside[u] - change[8 * u : 8 * u + 8, 128:256]
+        for u in range(t + 1, min(12, t + 3)):
             tail, more = rows[u], aside[u]
             raw, cols = [], []
             for l in range(8):
-                value = jnp.broadcast_to(tail[:, first + l : first + l + 1], (8, 128))
+                if u == t + 1 and t > 0:
+                    value = beyond[l]
+                else:
+                    value = jnp.broadcast_to(tail[:, first + l : first + l + 1], (8, 128))
                 for p in range(l):
                     value = value - cols[p] * cell[l, p]
                 raw.append(value)
                 cols.append(value * inv[l])
             if u == t + 1:
-                ahead = []
+                ahead, spread = [], {}
                 for m in range(8):
                     value = jnp.broadcast_to(tail[:, first + 8 + m : first + 9 + m], (8, 128))
                     for l in range(8):
-                        value = value - cols[l] * jnp.broadcast_to(raw[l][m : m + 1, :], (8, 128))
+                        spread[l, m] = jnp.broadcast_to(raw[l][m : m + 1, :], (8, 128))
+                        value = value - cols[l] * spread[l, m]
                     ahead.append(value)
+            if u == t + 2:
+                following = []
+                for m in range(8):
+                    value = jnp.broadcast_to(tail[:, first + 8 + m : first + 9 + m], (8, 128))
+                    for l in range(8):
+                        value = value - cols[l] * spread[l, m]
+                    following.append(value)
             for l in range(8):
                 tail = tail - cols[l] * line[l]
                 more = more - cols[l] * side[l]
             rows[u], aside[u] = tail, more
+        if t + 2 < 12:
+            beyond = following
     return jnp.concatenate(done, axis=0)
 
 
@@ -141,7 +164,7 @@
         lhs = jnp.concatenate([high, low], axis=1)
         return nt(lhs, jnp.concatenate([mhi, mhi], axis=1)) + nt(high, mlo)
 
-    keep(jnp.concatenate([start_ref[...], jnp.zeros((ROWS, 32), F32)], axis=1))
+    keep(start_ref[...])
     keep(times_gram())
 
     def step(_, carry):
@@ -150,8 +173,9 @@
         return carry
 
     lax.fori_loop(0, ITERS - 1, step, 0)
-    out = apply(zcat[0:ROWS, 0:128], zcat[0:ROWS, 128:256], factor())
-    out_ref[...] = out[:, 0:RANK]
+    high, low = split(factor())
+    z = zcat[0:ROWS]
+    out_ref[...] = nt(jnp.concatenate([high, high], axis=1), z) + nt(low, z[:, 0:128])
 
 
 def place():
@@ -330,7 +354,7 @@
     return has, which
 
 
-def first_gram(slab, xhi, xlo, rows, tiles, slab_send, more_send, slab_recv):
+def first_gram(slab, xhi, xlo, rows, tiles, slab_send, more_send, slab_recv, meanwhile):
     gx, gy, gz = lax.axis_index("gx"), lax.axis_index("gy"), lax.axis_index("gz")
     mine = pl.ds(gx * OWN, OWN)
     for e in range(5):
@@ -353,6 +377,7 @@
     local(slab.at[:, pl.ds(gx * 8, 8)], rows.at[0, mine], slab_recv.at[0])
 
     tiles[...] = jnp.zeros_like(tiles)
+    meanwhile()
 
     def use(p):
         for j in range(8):
@@ -371,15 +396,16 @@
     await_all(rows.at[0], slab_recv.at[0])
     use(0)
 
-    for c in copies:
-        c.wait_send()
-    for e in range(5):
-        to = extra_owner(gz, e)
-
-        @pl.when(to != gx)
-        def _():
-            src = slab.at[:, pl.ds(128 + 8 * e, 8)]
-            await_all(src, more_send.at[e])
+    def finish():
+        for c in copies:
+            c.wait_send()
+        for e in range(5):
+
+            @pl.when(extra_owner(gz, e) != gx)
+            def _():
+                await_all(slab.at[:, pl.ds(128 + 8 * e, 8)], more_send.at[e])
+
+    return finish
 
 
 def ranks(gy, core):
@@ -396,9 +422,7 @@
 
 
 def basis_rows(basis):
-    wide = jnp.concatenate([basis, jnp.zeros((ROWS, 32), F32)], axis=1)
-    high, low = split(wide.T[0:RANK])
-    return jnp.concatenate([high, low], axis=0)
+    return jnp.concatenate(split(basis), axis=0)
 
 
 def contract(stacked, hi, lo):
@@ -453,12 +477,6 @@
     @pl.when(held == 2)
     def _():
         await_all(rows, part_recv.at[0])
-        await_all(part.at[0, pl.ds(0, 94)], part_send.at[0])
-
-        @pl.when(has)
-        def _():
-            await_all(part.at[1, pl.ds(0, 94)], part_send.at[1])
-
         high, low = split(rows[1])
         qhi[:, 128:256] = high
         qlo[:, 128:256] = low
@@ -466,19 +484,26 @@
     @pl.when(held != 2)
     def _():
         await_all(rows.at[0], part_recv.at[0])
-        await_all(part.at[0, pl.ds(0, 95)], part_send.at[0])
-
-        @pl.when(has)
-        def _():
-            await_all(part.at[1, pl.ds(0, 95)], part_send.at[1])
-
         qhi[:, 128:256] = jnp.zeros((ROWS, 128), BF16)
         qlo[:, 128:256] = jnp.zeros((ROWS, 128), BF16)
+
+    def finish():
+        for count in (1, 2):
+
+            @pl.when(held == count)
+            def _():
+                sent = pl.ds(0, RANK - count)
+                await_all(part.at[0, sent], part_send.at[0])
+
+                @pl.when(has)
+                def _():
+                    await_all(part.at[1, sent], part_send.at[1])
 
     high, low = split(rows[0])
     qhi[:, 0:128] = high
     qlo[:, 0:128] = low
     add_gram(qhi, qlo, tiles, True)
+    return finish
 
 
 def core_piece(basis, qhi, qlo, out, terms, send, recv):
@@ -520,36 +545,52 @@
         pl.semaphore_signal(barrier, inc=1, device_id=to, device_id_type=MESH)
         return carry
 
-    lax.fori_loop(1, 64, hello, 0)
+    lax.fori_loop(32, 64, hello, 0)
+    lax.fori_loop(1, 32, hello, 0)
     ids = [device(x, y, z, 1 - core)] + [device(x, y, turn(z, d, 8), core) for d in (1, 3, 5, 7)]
     pl.semaphore_wait(barrier, 63 + greet(ids))
 
 
-def kernel(slab, start_one, start_two, factor_one, factor_two, core, xhi, xlo, columns, sums, part, rows, qhi, qlo,
+def kernel(slab, start_one, start_two, factor_one, factor_two, core, flat, starts, start_sem, xhi, xlo, columns, sums, part, rows, qhi, qlo,
            ghi, glo, zcat, terms, slab_send, more_send, slab_recv, part_send, part_recv, core_send, core_recv, *sum_refs):
     one, two = sum_refs[: len(SUM_SCRATCH)], sum_refs[len(SUM_SCRATCH) :]
+    pltpu.make_async_copy(start_one, flat.at[0], start_sem.at[0]).start()
+    pltpu.make_async_copy(start_two, flat.at[1], start_sem.at[1]).start()
     arrive()
-    first_gram(slab, xhi, xlo, columns, one[0], slab_send, more_send, slab_recv)
+
+    def turn_starts():
+        for n in range(2):
+            await_all(flat.at[n], start_sem.at[n])
+            wide = jnp.concatenate([flat[n], jnp.zeros((RANK, 96), F32)], axis=1)
+            wide = jnp.concatenate([wide, jnp.zeros((32, 768), F32)], axis=0)
+            starts[n] = wide.T[0:ROWS]
+
+    sent_slab = first_gram(slab, xhi, xlo, columns, one[0], slab_send, more_send, slab_recv, turn_starts)
     sum_everywhere(sums.at[0], *one)
-    subspace(1.0 / (ROWS * 512), sums.at[0], start_one, factor_one, ghi, glo, zcat)
-    second_gram(factor_one, xhi, xlo, qhi, qlo, part, rows, two[0], part_send, part_recv)
+    subspace(1.0 / (ROWS * 512), sums.at[0], starts.at[0], factor_one, ghi, glo, zcat)
+    sent_parts = second_gram(factor_one, xhi, xlo, qhi, qlo, part, rows, two[0], part_send, part_recv)
     sum_everywhere(sums.at[1], *two)
-    subspace(1.0 / (RANK * 512), sums.at[1], start_two, factor_two, ghi, glo, zcat)
+    subspace(1.0 / (RANK * 512), sums.at[1], starts.at[1], factor_two, ghi, glo, zcat)
     core_piece(factor_two, qhi, qlo, core, terms, core_send, core_recv)
+    sent_slab()
+    sent_parts()
 
 
 def body(slab, start_one, start_two):
     dma = pltpu.SemaphoreType.DMA
-    return pl.pallas_call(
+    one, two, core = pl.pallas_call(
         kernel,
         out_shape=(
-            jax.ShapeDtypeStruct((ROWS, RANK), F32),
-            jax.ShapeDtypeStruct((ROWS, RANK), F32),
+            jax.ShapeDtypeStruct((RANK, ROWS), F32),
+            jax.ShapeDtypeStruct((RANK, ROWS), F32),
             jax.ShapeDtypeStruct((6, 24, 128), F32),
         ),
-        in_specs=[pl.BlockSpec(memory_space=pltpu.MemorySpace.HBM), *vmem(2)],
+        in_specs=[pl.BlockSpec(memory_space=pltpu.MemorySpace.HBM)] * 3,
         out_specs=tuple(vmem(3)),
         scratch_shapes=[
+            pltpu.VMEM((2, RANK, ROWS), F32),
+            pltpu.VMEM((2, ROWS, 128), F32),
+            dma((2,)),
             pltpu.VMEM((2, ROWS, 1024), BF16),
             pltpu.VMEM((2, ROWS, 1024), BF16),
             pltpu.VMEM((2, ROWS, 8, 128), F32),
@@ -575,7 +616,8 @@
         compiler_params=pltpu.CompilerParams(
             collective_id=0, has_side_effects=True, vmem_limit_bytes=48 * 2**20),
         name="hosvd",
-    )(slab, start_one, start_two)
+    )(slab, start_one.T, start_two.T)
+    return one.T, two.T, core
 
 
 def solution(mesh):

time: 252 us -> 249 us (0.988)
  Pallas kernels: 245 us -> 242 us
    unnamed x5 -> x9, local copies, waits for them, and re-layouts: 4.91 us -> 6 us
where the time goes in v4:
time: 249 us
  Pallas kernels  242 us (97%)
  local copies, waits for them, and re-layouts  6 us (2%)
    pallas_call x1, Pallas kernels, body(): pl.pallas_call(kernel, out_shape=(jax.ShapeDtypeStruct((RANK, ROWS), F32)...  242 us
    unnamed x9, local copies, waits for them, and re-layouts  6 us

profile of v4, /device:TPU:1, one launch (start us, length us, event | category | flops | bytes accessed | tf_op | source)
XLA Modules:
  0.0 249.0 jit_solution(8541793740668552318)
XLA Ops:
  0.6 0.0 copy-start
  0.6 2.0 copy-done
  2.7 0.0 copy-start.1
  2.7 1.0 copy-done.1
  3.6 0.0 copy-start.2
  3.6 1.0 copy-done.2
  4.6 242.4 %hosvd.1 = (f32[96,672]{1,0:T(8,128)S(1)}, f32[96,672]{1,0:T(8,128)S(1)}, f32[6,24,128]{2,1,0:T(8,128)S(1)}) custom-call(f32[42,168,128]{2,1,0:T(8,128)S(1)} %copy-done, f32[96,672]{1,0:T(8,128)S(1)} %bitcast.4, f32[96,672]{1,0:T(8,128)S(1)} %bitcast.5), custom_call_target="tpu_custom_call" | custom-call | tf_op jit(solution)/shard_map/hosvd/pallas_call | solution.py:581
  246.9 0.7 copy.9
  247.7 0.7 copy.10
  248.4 0.6 copy.11
Async XLA Ops:
  0.6 2.0 copy-start
  2.7 1.0 copy-start.1
  3.6 1.0 copy-start.2
